TPU v7x, 32 devices: a whole 2x2x4 slice. The times are simulated.
32 devices in a mesh: gx: 8 (over z, core), gy: 4 (over y, x).
Axes of the slice: x: 2, y: 2, z: 4, core: 2. Of those that a mesh axis runs over, the one named last changes fastest.
Arguments:
- directions: float32 [16, 128, 128, 128], P(None, 'gx', 'gy'), may hold values from -6 to 6
- checkpoints: float32 [16, 128, 128, 128], P(None, 'gx', 'gy'), may hold values from -3 to 3
- restart: int32 [1], replicated, may hold values from 0 to 15
- diffusivity: float32 [128, 128, 128], P('gx', 'gy'), may hold values from 0.5 to 1.5
- velocity: float32 [3], replicated, may hold values from -0.4 to 0.4
- weights: float32 [128, 128, 128], P('gx', 'gy'), may hold values from 0.25 to 4
Outputs:
- basis: float32 [16, 128, 128, 128], P(None, 'gx', 'gy')
- factor: float32 [16, 16], replicated
All inputs are finite; a program needn't handle non-finite values.
Results may differ from a plain program's by a relative error of at most 0.0003.
Values sent between devices are 32-bit elements; how exact they have to be, the bound alone decides.
A program may use at most 128 MiB of HBM per device.

v0:
```python
import functools

import jax
import jax.numpy as jnp
from jax import lax
from jax.experimental import pallas as pl
from jax.experimental.pallas import tpu as pltpu
from jax.sharding import PartitionSpec as P

DIFFUSE = 0.1
REACT = 0.05
PRIOR = 0.25
GROUP = 4
MESH = pl.DeviceIdType.MESH
HIGHEST = lax.Precision.HIGHEST


def iota(shape, dim):
    return lax.broadcasted_iota(jnp.int32, shape, dim)


def sketch_kernel(
    nx, ny, cells,
    velocity, directions, start_in, diffusivity_in, weights_in,
    sketch, mixer, factor,
    f0, f1, f2, f3, pair, wts, ct, ca, c0s, c0l,
    ysend, yrecv, ypsend, yprecv, gram_x, gram_y,
    local_sem, send_sem, recv_sem, psend_sem, precv_sem, gsend_sem, grecv_sem,
):
    fields = (f0, f1, f2, f3)
    k_all, lx, ly, lz = sketch.shape
    tiles = ly // 8
    groups = k_all // GROUP
    gx, gy = lax.axis_index("gx"), lax.axis_index("gy")

    barrier = pltpu.get_barrier_semaphore()
    for axis, me, count in (("gx", gx, nx), ("gy", gy, ny)):
        for step in range(1, count):
            pl.semaphore_signal(
                barrier, inc=1, device_id={axis: lax.rem(me + step, count)}, device_id_type=MESH
            )

    def load_group(c):
        ks = pl.ds(c * GROUP, GROUP)
        return pltpu.make_async_copy(
            directions.at[ks], f0.at[ks, pl.ds(1, lx)], local_sem.at[c]
        )

    side_copies = (
        pltpu.make_async_copy(start_in, pair.at[0, pl.ds(1, lx)], local_sem.at[groups]),
        pltpu.make_async_copy(diffusivity_in, pair.at[1, pl.ds(1, lx)], local_sem.at[groups + 1]),
        pltpu.make_async_copy(weights_in, wts, local_sem.at[groups + 2]),
    )
    load_group(0).start()
    side_copies[0].start()
    side_copies[1].start()
    for c in range(1, groups):
        load_group(c).start()
    side_copies[2].start()

    plane_zero = jnp.zeros((ly, lz), jnp.float32)
    row_zero = jnp.zeros((lx, lz), jnp.float32)

    for edge, where in ((gx == 0, 0), (gx == nx - 1, lx + 1)):
        @pl.when(edge)
        def _(where=where):
            @pl.loop(0, k_all)
            def _(k):
                for field in fields:
                    field[k, where] = plane_zero
            for k in range(2):
                pair[k, where] = plane_zero

    for edge, side in ((gy == 0, 0), (gy == ny - 1, 1)):
        @pl.when(edge)
        def _(side=side):
            @pl.loop(0, k_all)
            def _(k):
                for stage in range(4):
                    yrecv[stage, side, k] = row_zero
            for k in range(2):
                yprecv[side, k] = row_zero

    def routes(planes, ys, yr, ks, send, recv):
        def copy(src, dst, side, peer):
            return pltpu.make_async_remote_copy(
                src_ref=src, dst_ref=dst, send_sem=send(side), recv_sem=recv(side),
                device_id=peer, device_id_type=MESH,
            )
        return (
            (gx < nx - 1, gx > 0, copy(planes.at[ks, lx], planes.at[ks, 0], 0, {"gx": lax.rem(gx + 1, nx)})),
            (gx > 0, gx < nx - 1, copy(planes.at[ks, 1], planes.at[ks, lx + 1], 1, {"gx": lax.rem(gx + nx - 1, nx)})),
            (gy < ny - 1, gy > 0, copy(ys.at[0, ks], yr.at[0, ks], 2, {"gy": lax.rem(gy + 1, ny)})),
            (gy > 0, gy < ny - 1, copy(ys.at[1, ks], yr.at[1, ks], 3, {"gy": lax.rem(gy + ny - 1, ny)})),
        )

    def stage_routes(stage, c):
        return routes(
            fields[stage], ysend.at[stage], yrecv.at[stage], pl.ds(c * GROUP, GROUP),
            lambda side: send_sem.at[stage, side, c], lambda side: recv_sem.at[stage, side, c],
        )

    def pair_routes():
        return routes(
            pair, ypsend, yprecv, pl.ds(0, 2),
            lambda side: psend_sem.at[side], lambda side: precv_sem.at[side],
        )

    def send_all(ways):
        for sends, _, copy in ways:
            pl.when(sends)(copy.start)

    def recv_all(ways):
        for _, receives, copy in ways:
            pl.when(receives)(copy.wait_recv)

    def sent_all(ways):
        for sends, _, copy in ways:
            pl.when(sends)(copy.wait_send)

    row = iota((8, lz), 0)
    lane = iota((8, lz), 1)
    hx, hy, hz = (0.5 * velocity[i] for i in range(3))

    def around(field, yr, k, x, t):
        p = x + 1
        lo = t * 8
        middle = field[k, p, lo:lo + 8, :]
        east = field[k, p + 1, lo:lo + 8, :]
        west = field[k, p - 1, lo:lo + 8, :]
        if t < tiles - 1:
            north = field[k, p, lo + 1:lo + 9, :]
        else:
            north = jnp.where(row == 7, yr[1, k, pl.ds(x, 1), :], pltpu.roll(middle, 7, 0))
        if t > 0:
            south = field[k, p, lo - 1:lo + 7, :]
        else:
            south = jnp.where(row == 0, yr[0, k, pl.ds(x, 1), :], pltpu.roll(middle, 1, 0))
        upper = pltpu.roll(middle, lz - 1, 1)
        lower = pltpu.roll(middle, 1, 1)
        return middle, (east, west, north, south, upper, lower)

    def weighted(c0, cs, middle, sides):
        terms = [c * v for c, v in zip(cs, sides)]
        return ((terms[0] + terms[1]) + (terms[2] + terms[3])) + ((terms[4] + terms[5]) + c0 * middle)

    def pack_group(c):
        @pl.loop(0, lx)
        def _(x):
            for i in range(GROUP):
                k = c * GROUP + i
                ysend[0, 0, k, pl.ds(x, 1), :] = f0[k, x + 1, ly - 1:ly, :]
                ysend[0, 1, k, pl.ds(x, 1), :] = f0[k, x + 1, 0:1, :]

    load_group(0).wait()
    pack_group(0)
    side_copies[0].wait()
    side_copies[1].wait()

    @pl.loop(0, lx)
    def _(x):
        for k in range(2):
            ypsend[0, k, pl.ds(x, 1), :] = pair[k, x + 1, ly - 1:ly, :]
            ypsend[1, k, pl.ds(x, 1), :] = pair[k, x + 1, 0:1, :]

    pl.semaphore_wait(barrier, nx + ny - 2)
    send_all(stage_routes(0, 0))
    send_all(pair_routes())

    @pl.loop(1, groups)
    def _(c):
        load_group(c).wait()
        pack_group(c)
        send_all(stage_routes(0, c))

    @pl.loop(0, lx)
    def _(x):
        for t in range(tiles):
            rows = slice(t * 8, t * 8 + 8)
            a = DIFFUSE * pair[1, x + 1, rows, :]
            state = pair[0, x + 1, rows, :]
            ct[0, x, rows, :] = a - hx
            ct[1, x, rows, :] = a + hx
            ct[2, x, rows, :] = a - hy
            ct[3, x, rows, :] = a + hy
            ct[4, x, rows, :] = jnp.where(lane < lz - 1, a - hz, 0.0)
            ct[5, x, rows, :] = jnp.where(lane > 0, a + hz, 0.0)
            c0s[x, rows, :] = 1.0 - 6.0 * a - (3.0 * REACT) * state * state

    def run_stage(stage, coefs, centre, finish, out):
        field = fields[stage]
        last = stage == 3

        @pl.loop(0, groups)
        def _(c):
            recv_all(stage_routes(stage, c))

            @pl.loop(0, lx)
            def _(x):
                for t in range(tiles):
                    rows = slice(t * 8, t * 8 + 8)
                    cs = [coefs[i, x, rows, :] for i in range(6)]
                    c0 = centre[x, rows, :]
                    extra = wts[x, rows, :] if finish == "weights" else None
                    for i in range(GROUP):
                        k = c * GROUP + i
                        middle, sides = around(field, yrecv.at[stage], k, x, t)
                        value = weighted(c0, cs, middle, sides)
                        if finish == "weights":
                            value = extra * value
                        if finish == "prior":
                            value = value + PRIOR * f0[k, x + 1, rows, :]
                        if last:
                            out[k, x, rows, :] = value
                        else:
                            out[k, x + 1, rows, :] = value
                            if t == tiles - 1:
                                ysend[stage + 1, 0, k, pl.ds(x, 1), :] = value[7:8, :]
                            if t == 0:
                                ysend[stage + 1, 1, k, pl.ds(x, 1), :] = value[0:1, :]

            if not last:
                send_all(stage_routes(stage + 1, c))

    run_stage(0, ct, c0s, None, f1)

    recv_all(pair_routes())
    side_copies[2].wait()

    @pl.loop(0, lx)
    def _(x):
        for t in range(tiles):
            rows = slice(t * 8, t * 8 + 8)
            state, sides = around(pair, yprecv, 0, x, t)
            cs = [ct[i, x, rows, :] for i in range(6)]
            diff, around_diff = around(pair, yprecv, 1, x, t)
            plain = 1.0 - (6.0 * DIFFUSE) * diff
            later = weighted(plain - REACT * state * state, cs, state, sides)
            c0l[x, rows, :] = plain - (3.0 * REACT) * later * later
            for i, (speed, other) in enumerate(zip((hx, -hx, hy, -hy, hz, -hz), around_diff)):
                value = DIFFUSE * other + speed
                if i == 4:
                    value = jnp.where(lane < lz - 1, value, 0.0)
                if i == 5:
                    value = jnp.where(lane > 0, value, 0.0)
                ca[i, x, rows, :] = value

    run_stage(1, ct, c0l, "weights", f2)
    run_stage(2, ca, c0l, None, f3)
    run_stage(3, ca, c0s, "prior", sketch)

    side = k_all * 8

    def products(x, total):
        block = jnp.concatenate(
            [sketch[:, x, t * 8:t * 8 + 8, :].reshape(side, lz) for t in range(tiles)], axis=1
        )
        high = block.astype(jnp.bfloat16)
        low = (block - high.astype(jnp.float32)).astype(jnp.bfloat16)
        return total + lax.dot_general(
            high, jnp.concatenate([high, low], axis=0), (((1,), (1,)), ((), ())),
            preferred_element_type=jnp.float32,
        )

    total = lax.fori_loop(0, lx, products, jnp.zeros((side, 2 * side), jnp.float32))
    low_part = total[:, side:]
    whole = total[:, :side] + low_part + low_part.T
    r_big, c_big = iota((side, side), 0), iota((side, side), 1)
    same_y = (r_big & 7) == (c_big & 7)
    whole = jnp.where(same_y, whole, 0.0)
    fold = (iota((k_all, side), 0) == iota((k_all, side), 1) >> 3).astype(jnp.float32)
    folded = jnp.dot(fold, whole, precision=HIGHEST, preferred_element_type=jnp.float32)

    for axis, me, count, slots, at in (("gx", gx, nx, gram_x, 0), ("gy", gy, ny, gram_y, nx)):
        slots[me] = folded
        copies = []
        for step in range(1, count):
            peer = lax.rem(me + step, count)
            copies.append(pltpu.make_async_remote_copy(
                src_ref=slots.at[me], dst_ref=slots.at[me],
                send_sem=gsend_sem.at[at + step], recv_sem=grecv_sem.at[at + me],
                device_id={axis: peer}, device_id_type=MESH,
            ))
        for copy in copies:
            copy.start()
        for step in range(1, count):
            peer = lax.rem(me + step, count)
            pltpu.make_async_remote_copy(
                src_ref=slots.at[peer], dst_ref=slots.at[peer],
                send_sem=gsend_sem.at[at + step], recv_sem=grecv_sem.at[at + peer],
                device_id={axis: peer}, device_id_type=MESH,
            ).wait_recv()
        folded = slots[0]
        for i in range(1, count):
            folded = folded + slots[i]
        for copy in copies:
            copy.wait_send()

    pick = (iota((side, lz), 0) >> 3 == iota((side, lz), 1)).astype(jnp.float32)
    work = jnp.dot(folded * (1.0 / cells), pick, precision=HIGHEST, preferred_element_type=jnp.float32)
    kr, kc = iota((k_all, lz), 0), iota((k_all, lz), 1)
    work = work + (kc == kr + k_all).astype(jnp.float32)
    for j in range(k_all - 1):
        ratio = jnp.where(kr > j, work[:, j:j + 1] / work[j:j + 1, j:j + 1], 0.0)
        work = work - ratio * work[j:j + 1, :]
    diagonal = jnp.sum(jnp.where(kr == kc, work, 0.0), axis=1, keepdims=True)
    work = work / jnp.sqrt(diagonal)
    factor[...] = jnp.where(kc >= kr, work, 0.0)[:, :k_all]
    spread = (iota((lz, side), 0) == (iota((lz, side), 1) >> 3) + k_all).astype(jnp.float32)
    inverse = jnp.dot(work, spread, precision=HIGHEST, preferred_element_type=jnp.float32)
    unfold = (iota((side, k_all), 0) >> 3 == iota((side, k_all), 1)).astype(jnp.float32)
    inverse = jnp.dot(unfold, inverse, precision=HIGHEST, preferred_element_type=jnp.float32)
    inverse = jnp.where(same_y, inverse, 0.0)
    high = inverse.astype(jnp.bfloat16)
    low = (inverse - high.astype(jnp.float32)).astype(jnp.bfloat16)
    mixer[:side, :side] = high
    mixer[:side, side:] = high
    mixer[side:, :side] = low
    mixer[side:, side:] = jnp.zeros_like(low)

    @pl.loop(0, groups)
    def _(c):
        for stage in range(4):
            sent_all(stage_routes(stage, c))
    sent_all(pair_routes())


def basis_kernel(mixer, sketch, basis):
    planes = basis.shape[1]
    k_all, _, ly, lz = sketch.shape
    tiles = ly // 8
    side = k_all * 8
    base = pl.program_id(0) * planes
    for i in range(planes):
        block = jnp.concatenate(
            [sketch[:, base + i, t * 8:t * 8 + 8, :].reshape(side, lz) for t in range(tiles)], axis=1
        )
        high = block.astype(jnp.bfloat16)
        low = (block - high.astype(jnp.float32)).astype(jnp.bfloat16)
        both = jnp.dot(
            mixer[...], jnp.concatenate([high, low], axis=0), preferred_element_type=jnp.float32
        )
        result = both[:side] + both[side:]
        for t in range(tiles):
            basis[:, i, t * 8:t * 8 + 8, :] = result[:, t * lz:(t + 1) * lz].reshape(k_all, 8, lz)


def local(nx, ny, directions, checkpoints, restart, diffusivity, velocity, weights):
    k_all, lx, ly, lz = directions.shape
    start = lax.dynamic_index_in_dim(checkpoints, restart[0], 0, keepdims=False)
    side = 8 * k_all
    groups = k_all // GROUP
    f32 = jnp.float32
    vmem = pl.BlockSpec(memory_space=pltpu.VMEM)
    anywhere = pl.BlockSpec(memory_space=pl.ANY)
    field = pltpu.VMEM((k_all, lx + 2, ly, lz), f32)
    cell = pltpu.VMEM((lx, ly, lz), f32)
    dma = pltpu.SemaphoreType.DMA
    sketch, mixer, factor = pl.pallas_call(
        functools.partial(sketch_kernel, nx, ny, float(nx * ny * lx * ly * lz)),
        out_shape=(
            pltpu.VMEM(directions.shape, f32),
            pltpu.VMEM((2 * side, 2 * side), jnp.bfloat16),
            jax.ShapeDtypeStruct((k_all, k_all), f32),
        ),
        in_specs=[pl.BlockSpec(memory_space=pltpu.SMEM)] + [anywhere] * 4,
        out_specs=(vmem, vmem, vmem),
        scratch_shapes=[
            field, field, field, field,
            pltpu.VMEM((2, lx + 2, ly, lz), f32),
            cell,
            pltpu.VMEM((6, lx, ly, lz), f32),
            pltpu.VMEM((6, lx, ly, lz), f32),
            cell, cell,
            pltpu.VMEM((4, 2, k_all, lx, lz), f32),
            pltpu.VMEM((4, 2, k_all, lx, lz), f32),
            pltpu.VMEM((2, 2, lx, lz), f32),
            pltpu.VMEM((2, 2, lx, lz), f32),
            pltpu.VMEM((nx, k_all, side), f32),
            pltpu.VMEM((ny, k_all, side), f32),
            dma((groups + 3,)),
            dma((4, 4, groups)),
            dma((4, 4, groups)),
            dma((4,)),
            dma((4,)),
            dma((nx + ny,)),
            dma((nx + ny,)),
        ],
        compiler_params=pltpu.CompilerParams(
            collective_id=0, has_side_effects=True, vmem_limit_bytes=48 * 2**20
        ),
        name="sketch",
    )(velocity, directions, start, diffusivity, weights)
    planes = 2
    basis = pl.pallas_call(
        basis_kernel,
        out_shape=jax.ShapeDtypeStruct(directions.shape, f32),
        grid=(lx // planes,),
        in_specs=[vmem, vmem],
        out_specs=pl.BlockSpec((k_all, planes, ly, lz), lambda i: (0, i, 0, 0)),
        compiler_params=pltpu.CompilerParams(vmem_limit_bytes=48 * 2**20),
        name="basis",
    )(mixer, sketch)
    return basis, factor


def solution(mesh):
    placed = (
        P(None, "gx", "gy", None),
        P(None, "gx", "gy", None),
        P(),
        P("gx", "gy", None),
        P(),
        P("gx", "gy", None),
    )
    return jax.shard_map(
        functools.partial(local, mesh.shape["gx"], mesh.shape["gy"]),
        mesh=mesh,
        in_specs=placed,
        out_specs=(P(None, "gx", "gy", None), P()),
        check_vma=False,
    )
```

profile of v0, /device:TPU:0, one launch (start us, length us, event | category | flops | bytes accessed | tf_op | source)
XLA Modules:
  0.0 63.8 jit_solution(11704281243221378351)
XLA Ops:
  1.3 1.0 %dynamic-slice_bitcast_fusion.start_in = f32[16,32,128]{2,1,0:T(8,128)S(1)} fusion(f32[16,16,32,128]{3,2,1,0:T(8,128)} %param.7, s32[]{:T(128)S(6)} %select_n.4), kind=kLoop, calls=%fused_computation | loop fusion | bytes 524292 | tf_op jit(solution)/shard_map/jit(dynamic_index_in_dim)/squeeze | solution.py:350
  2.3 0.0 copy-start
  2.3 0.9 %copy-done = f32[16,32,128]{2,1,0:T(8,128)S(1)} copy-done((f32[16,32,128]{2,1,0:T(8,128)S(1)}, f32[16,32,128]{2,1,0:T(8,128)}, u32[]{:S(2)}) %copy-start) | copy-done | bytes 262168
  3.2 0.0 copy-start.1
  3.2 0.9 %copy-done.1 = f32[16,32,128]{2,1,0:T(8,128)S(1)} copy-done((f32[16,32,128]{2,1,0:T(8,128)S(1)}, f32[16,32,128]{2,1,0:T(8,128)}, u32[]{:S(2)}) %copy-start.1) | copy-done | bytes 262168
  4.2 0.0 copy-start.2
  4.2 0.7 %copy-done.2 = f32[3]{0:T(128)S(1)} copy-done((f32[3]{0:T(128)S(1)}, f32[3]{0:T(128)}, u32[]{:S(2)}) %copy-start.2) | copy-done | bytes 36
  4.8 53.6 %sketch.1 = (f32[16,16,32,128]{3,2,1,0:T(8,128)S(1)}, bf16[256,256]{1,0:T(8,128)(2,1)S(1)}, f32[16,16]{1,0:T(8,128)S(1)}) custom-call(f32[3]{0:T(128)S(1)} %copy-done.2, f32[16,16,32,128]{3,2,1,0:T(8,128)} %directions.1, f32[16,32,128]{2,1,0:T(8,128)S(1)} %dynamic-slice_bitcast_fusion.start_in, f32[16,32,128]{2,1,0:T(8,128)S(1)} %copy-done, ...), custom_call_target="tpu_custom_call" | custom-call | tf_op jit(solution)/shard_map/sketch/pallas_call | solution.py:359
  58.4 4.8 %basis.1 = f32[16,16,32,128]{3,2,1,0:T(8,128)} custom-call(bf16[256,256]{1,0:T(8,128)(2,1)S(1)} %get-tuple-element.5.mixer, f32[16,16,32,128]{3,2,1,0:T(8,128)S(1)} %get-tuple-element.6.sketch), custom_call_target="tpu_custom_call" | custom-call | tf_op jit(solution)/shard_map/basis/pallas_call | solution.py:395
  63.2 0.6 copy.10
Async XLA Ops:
  2.3 1.0 %copy-start = (f32[16,32,128]{2,1,0:T(8,128)S(1)}, f32[16,32,128]{2,1,0:T(8,128)}, u32[]{:S(2)}) copy-start(f32[16,32,128]{2,1,0:T(8,128)} %diffusivity_in.1) | copy-start | bytes 786436
  3.2 0.9 %copy-start.1 = (f32[16,32,128]{2,1,0:T(8,128)S(1)}, f32[16,32,128]{2,1,0:T(8,128)}, u32[]{:S(2)}) copy-start(f32[16,32,128]{2,1,0:T(8,128)} %weights_in.1) | copy-start | bytes 786436
  4.2 0.7 %copy-start.2 = (f32[3]{0:T(128)S(1)}, f32[3]{0:T(128)}, u32[]{:S(2)}) copy-start(f32[3]{0:T(128)} %velocity.1) | copy-start | bytes 40
where the time goes:
time: 64 us; the launch traced here: 63.8 us
  Pallas kernels  58.3 us (91%)
  local copies, waits for them, and re-layouts  4.12 us (6%)
  between operations  1.3 us (2%)
    pallas_call x1, Pallas kernels, local(): pl.pallas_call(functools.partial(sketch_kernel, nx, ny, float(nx * ny * l...  53.6 us
    pallas_call x1, Pallas kernels, local(): pl.pallas_call(basis_kernel, out_shape=jax.ShapeDtypeStruct(directions.sh...  4.79 us
    unnamed x7, local copies, waits for them, and re-layouts  3.15 us

commit v1 on v0

--- a/solution.py
+++ b/solution.py
@@ -21,9 +21,9 @@
 
 def sketch_kernel(
     nx, ny, cells,
-    velocity, directions, start_in, diffusivity_in, weights_in,
+    velocity, restart, directions, checkpoints, diffusivity_in, weights_in,
     sketch, mixer, factor,
-    f0, f1, f2, f3, pair, wts, ct, ca, c0s, c0l,
+    f0, f1, f2, f3, pair, saved, wts, ct, ca, c0s, c0l,
     ysend, yrecv, ypsend, yprecv, gram_x, gram_y,
     local_sem, send_sem, recv_sem, psend_sem, precv_sem, gsend_sem, grecv_sem,
 ):
@@ -47,16 +47,16 @@
         )
 
     side_copies = (
-        pltpu.make_async_copy(start_in, pair.at[0, pl.ds(1, lx)], local_sem.at[groups]),
+        pltpu.make_async_copy(checkpoints, saved, local_sem.at[groups]),
         pltpu.make_async_copy(diffusivity_in, pair.at[1, pl.ds(1, lx)], local_sem.at[groups + 1]),
         pltpu.make_async_copy(weights_in, wts, local_sem.at[groups + 2]),
     )
     load_group(0).start()
     side_copies[0].start()
     side_copies[1].start()
+    side_copies[2].start()
     for c in range(1, groups):
         load_group(c).start()
-    side_copies[2].start()
 
     plane_zero = jnp.zeros((ly, lz), jnp.float32)
     row_zero = jnp.zeros((lx, lz), jnp.float32)
@@ -157,8 +157,11 @@
     side_copies[0].wait()
     side_copies[1].wait()
 
+    first_state = restart[0]
+
     @pl.loop(0, lx)
     def _(x):
+        pair[0, x + 1] = saved[first_state, x]
         for k in range(2):
             ypsend[0, k, pl.ds(x, 1), :] = pair[k, x + 1, ly - 1:ly, :]
             ypsend[1, k, pl.ds(x, 1), :] = pair[k, x + 1, 0:1, :]
@@ -173,20 +176,6 @@
         pack_group(c)
         send_all(stage_routes(0, c))
 
-    @pl.loop(0, lx)
-    def _(x):
-        for t in range(tiles):
-            rows = slice(t * 8, t * 8 + 8)
-            a = DIFFUSE * pair[1, x + 1, rows, :]
-            state = pair[0, x + 1, rows, :]
-            ct[0, x, rows, :] = a - hx
-            ct[1, x, rows, :] = a + hx
-            ct[2, x, rows, :] = a - hy
-            ct[3, x, rows, :] = a + hy
-            ct[4, x, rows, :] = jnp.where(lane < lz - 1, a - hz, 0.0)
-            ct[5, x, rows, :] = jnp.where(lane > 0, a + hz, 0.0)
-            c0s[x, rows, :] = 1.0 - 6.0 * a - (3.0 * REACT) * state * state
-
     def run_stage(stage, coefs, centre, finish, out):
         field = fields[stage]
         last = stage == 3
@@ -195,7 +184,7 @@
         def _(c):
             recv_all(stage_routes(stage, c))
 
-            @pl.loop(0, lx)
+            @pl.loop(0, lx, unroll=8)
             def _(x):
                 for t in range(tiles):
                     rows = slice(t * 8, t * 8 + 8)
@@ -222,6 +211,20 @@
             if not last:
                 send_all(stage_routes(stage + 1, c))
 
+    @pl.loop(0, lx)
+    def _(x):
+        for t in range(tiles):
+            rows = slice(t * 8, t * 8 + 8)
+            a = DIFFUSE * pair[1, x + 1, rows, :]
+            state = pair[0, x + 1, rows, :]
+            ct[0, x, rows, :] = a - hx
+            ct[1, x, rows, :] = a + hx
+            ct[2, x, rows, :] = a - hy
+            ct[3, x, rows, :] = a + hy
+            ct[4, x, rows, :] = jnp.where(lane < lz - 1, a - hz, 0.0)
+            ct[5, x, rows, :] = jnp.where(lane > 0, a + hz, 0.0)
+            c0s[x, rows, :] = 1.0 - 6.0 * a - (3.0 * REACT) * state * state
+
     run_stage(0, ct, c0s, None, f1)
 
     recv_all(pair_routes())
@@ -262,7 +265,7 @@
             preferred_element_type=jnp.float32,
         )
 
-    total = lax.fori_loop(0, lx, products, jnp.zeros((side, 2 * side), jnp.float32))
+    total = lax.fori_loop(0, lx, products, jnp.zeros((side, 2 * side), jnp.float32), unroll=4)
     low_part = total[:, side:]
     whole = total[:, :side] + low_part + low_part.T
     r_big, c_big = iota((side, side), 0), iota((side, side), 1)
@@ -347,12 +350,12 @@
 
 def local(nx, ny, directions, checkpoints, restart, diffusivity, velocity, weights):
     k_all, lx, ly, lz = directions.shape
-    start = lax.dynamic_index_in_dim(checkpoints, restart[0], 0, keepdims=False)
     side = 8 * k_all
     groups = k_all // GROUP
     f32 = jnp.float32
     vmem = pl.BlockSpec(memory_space=pltpu.VMEM)
-    anywhere = pl.BlockSpec(memory_space=pl.ANY)
+    scalars = pl.BlockSpec(memory_space=pltpu.SMEM)
+    hbm = pl.BlockSpec(memory_space=pltpu.HBM)
     field = pltpu.VMEM((k_all, lx + 2, ly, lz), f32)
     cell = pltpu.VMEM((lx, ly, lz), f32)
     dma = pltpu.SemaphoreType.DMA
@@ -363,11 +366,12 @@
             pltpu.VMEM((2 * side, 2 * side), jnp.bfloat16),
             jax.ShapeDtypeStruct((k_all, k_all), f32),
         ),
-        in_specs=[pl.BlockSpec(memory_space=pltpu.SMEM)] + [anywhere] * 4,
+        in_specs=[scalars] * 2 + [hbm] * 4,
         out_specs=(vmem, vmem, vmem),
         scratch_shapes=[
             field, field, field, field,
             pltpu.VMEM((2, lx + 2, ly, lz), f32),
+            pltpu.VMEM(checkpoints.shape, f32),
             cell,
             pltpu.VMEM((6, lx, ly, lz), f32),
             pltpu.VMEM((6, lx, ly, lz), f32),
@@ -387,11 +391,11 @@
             dma((nx + ny,)),
         ],
         compiler_params=pltpu.CompilerParams(
-            collective_id=0, has_side_effects=True, vmem_limit_bytes=48 * 2**20
+            collective_id=0, has_side_effects=True, vmem_limit_bytes=239 * 2**18
         ),
         name="sketch",
-    )(velocity, directions, start, diffusivity, weights)
-    planes = 2
+    )(velocity, restart, directions, checkpoints, diffusivity, weights)
+    planes = 4
     basis = pl.pallas_call(
         basis_kernel,
         out_shape=jax.ShapeDtypeStruct(directions.shape, f32),

time: 64 us -> 51.1 us (0.80)
  Pallas kernels: 58.3 us -> 49.1 us
  local copies, waits for them, and re-layouts: 4.12 us -> 0.6 us
    pallas_call x1, Pallas kernels: 53.6 us -> 45.8 us  [local(): pl.pallas_call(functools.partial(sketch_kernel, nx, ny, float(nx * ny * l...]
    unnamed x7 -> x3, local copies, waits for them, and re-layouts: 3.15 us -> 0.6 us
    pallas_call x1, Pallas kernels: 4.79 us -> 3.3 us  [local(): pl.pallas_call(basis_kernel, out_shape=jax.ShapeDtypeStruct(directions.sh...]
    squeeze x1 -> x0, local copies, waits for them, and re-layouts: 0.97 us -> none  [local(): start = lax.dynamic_index_in_dim(checkpoints, restart[0], 0, keepdims=False)]
where the time goes in v1:
time: 51.1 us; the launch traced here: 51 us
  Pallas kernels  49.1 us (96%)
  between operations  1.29 us (3%)
  local copies, waits for them, and re-layouts  0.6 us (1%)
    pallas_call x1, Pallas kernels, local(): pl.pallas_call(functools.partial(sketch_kernel, nx, ny, float(nx * ny * l...  45.8 us
    pallas_call x1, Pallas kernels, local(): pl.pallas_call(basis_kernel, out_shape=jax.ShapeDtypeStruct(directions.sh...  3.3 us

profile of v1, /device:TPU:0, one launch (start us, length us, event | category | flops | bytes accessed | tf_op | source)
XLA Modules:
  0.0 51.0 jit_solution(1324945399494044766)
XLA Ops:
  1.3 45.8 %sketch.1 = (f32[16,16,32,128]{3,2,1,0:T(8,128)S(1)}, bf16[256,256]{1,0:T(8,128)(2,1)S(1)}, f32[16,16]{1,0:T(8,128)}) custom-call(f32[3]{0:T(128)} %velocity.1, s32[1]{0:T(128)S(6)} %copy.9.restart, f32[16,16,32,128]{3,2,1,0:T(8,128)} %directions.1, f32[16,16,32,128]{3,2,1,0:T(8,128)} %checkpoints.1, f32[16,32,128]{2,1,0:T(8,128)} %diffusivity_in.1, ...), custom_call_target="tpu_custom_call" | custom-call | tf_op jit(solution)/shard_map/sketch/pallas_call | solution.py:362
  47.1 0.0 copy-start
  47.1 3.3 %basis.1 = f32[16,16,32,128]{3,2,1,0:T(8,128)} custom-call(bf16[256,256]{1,0:T(8,128)(2,1)S(1)} %get-tuple-element.5.mixer, f32[16,16,32,128]{3,2,1,0:T(8,128)S(1)} %get-tuple-element.6.sketch), custom_call_target="tpu_custom_call" | custom-call | tf_op jit(solution)/shard_map/basis/pallas_call | solution.py:399
  50.4 0.0 copy-done
  50.4 0.6 %copy.10 = f32[16,16]{1,0:T(8,128)} copy(f32[16,16]{1,0:T(8,128)S(1)} %copy-done) | data formatting | bytes 2048
Async XLA Ops:
  47.1 3.3 %copy-start = (f32[16,16]{1,0:T(8,128)S(1)}, f32[16,16]{1,0:T(8,128)}, u32[]{:S(2)}) copy-start(f32[16,16]{1,0:T(8,128)} %get-tuple-element.11) | copy-start | bytes 3076

commit v2 on v1

--- a/solution.py
+++ b/solution.py
@@ -51,12 +51,10 @@
         pltpu.make_async_copy(diffusivity_in, pair.at[1, pl.ds(1, lx)], local_sem.at[groups + 1]),
         pltpu.make_async_copy(weights_in, wts, local_sem.at[groups + 2]),
     )
-    load_group(0).start()
-    side_copies[0].start()
-    side_copies[1].start()
-    side_copies[2].start()
-    for c in range(1, groups):
+    for c in range(groups):
         load_group(c).start()
+    for copy in (side_copies[1], side_copies[0], side_copies[2]):
+        copy.start()
 
     plane_zero = jnp.zeros((ly, lz), jnp.float32)
     row_zero = jnp.zeros((lx, lz), jnp.float32)
@@ -154,21 +152,8 @@
 
     load_group(0).wait()
     pack_group(0)
-    side_copies[0].wait()
-    side_copies[1].wait()
-
-    first_state = restart[0]
-
-    @pl.loop(0, lx)
-    def _(x):
-        pair[0, x + 1] = saved[first_state, x]
-        for k in range(2):
-            ypsend[0, k, pl.ds(x, 1), :] = pair[k, x + 1, ly - 1:ly, :]
-            ypsend[1, k, pl.ds(x, 1), :] = pair[k, x + 1, 0:1, :]
-
     pl.semaphore_wait(barrier, nx + ny - 2)
     send_all(stage_routes(0, 0))
-    send_all(pair_routes())
 
     @pl.loop(1, groups)
     def _(c):
@@ -210,6 +195,20 @@
 
             if not last:
                 send_all(stage_routes(stage + 1, c))
+
+    side_copies[0].wait()
+    side_copies[1].wait()
+
+    first_state = restart[0]
+
+    @pl.loop(0, lx)
+    def _(x):
+        pair[0, x + 1] = saved[first_state, x]
+        for k in range(2):
+            ypsend[0, k, pl.ds(x, 1), :] = pair[k, x + 1, ly - 1:ly, :]
+            ypsend[1, k, pl.ds(x, 1), :] = pair[k, x + 1, 0:1, :]
+
+    send_all(pair_routes())
 
     @pl.loop(0, lx)
     def _(x):

time: 51.1 us -> 49.8 us (0.975)
  Pallas kernels: 49.1 us -> 47.8 us
    pallas_call x1, Pallas kernels: 45.8 us -> 44.5 us  [local(): pl.pallas_call(functools.partial(sketch_kernel, nx, ny, float(nx * ny * l...]
where the time goes in v2:
time: 49.8 us; the launch traced here: 49.7 us
  Pallas kernels  47.8 us (96%)
  between operations  1.29 us (3%)
  local copies, waits for them, and re-layouts  0.6 us (1%)
    pallas_call x1, Pallas kernels, local(): pl.pallas_call(functools.partial(sketch_kernel, nx, ny, float(nx * ny * l...  44.5 us
    pallas_call x1, Pallas kernels, local(): pl.pallas_call(basis_kernel, out_shape=jax.ShapeDtypeStruct(directions.sh...  3.3 us

profile of v2, /device:TPU:0, one launch (start us, length us, event | category | flops | bytes accessed | tf_op | source)
XLA Modules:
  0.0 49.7 jit_solution(15426779357705629182)
XLA Ops:
  1.3 44.5 %sketch.1 = (f32[16,16,32,128]{3,2,1,0:T(8,128)S(1)}, bf16[256,256]{1,0:T(8,128)(2,1)S(1)}, f32[16,16]{1,0:T(8,128)}) custom-call(f32[3]{0:T(128)} %velocity.1, s32[1]{0:T(128)S(6)} %copy.9.restart, f32[16,16,32,128]{3,2,1,0:T(8,128)} %directions.1, f32[16,16,32,128]{3,2,1,0:T(8,128)} %checkpoints.1, f32[16,32,128]{2,1,0:T(8,128)} %diffusivity_in.1, ...), custom_call_target="tpu_custom_call" | custom-call | tf_op jit(solution)/shard_map/sketch/pallas_call | solution.py:361
  45.7 0.0 copy-start
  45.8 3.3 %basis.1 = f32[16,16,32,128]{3,2,1,0:T(8,128)} custom-call(bf16[256,256]{1,0:T(8,128)(2,1)S(1)} %get-tuple-element.5.mixer, f32[16,16,32,128]{3,2,1,0:T(8,128)S(1)} %get-tuple-element.6.sketch), custom_call_target="tpu_custom_call" | custom-call | tf_op jit(solution)/shard_map/basis/pallas_call | solution.py:398
  49.1 0.0 copy-done
  49.1 0.6 %copy.10 = f32[16,16]{1,0:T(8,128)} copy(f32[16,16]{1,0:T(8,128)S(1)} %copy-done) | data formatting | bytes 2048
Async XLA Ops:
  45.7 3.3 %copy-start = (f32[16,16]{1,0:T(8,128)S(1)}, f32[16,16]{1,0:T(8,128)}, u32[]{:S(2)}) copy-start(f32[16,16]{1,0:T(8,128)} %get-tuple-element.11) | copy-start | bytes 3076
